TPU v7x, 1024 devices: a whole 4x8x16 slice. The times are simulated.
1024 devices in a mesh: row: 16 (over z_lo, x), col: 64 (over y, z_hi, core).
Axes of the slice: x: 4, y: 8, z: 16 (z_hi: 4, z_lo: 4; z = z_hi * 4 + z_lo), core: 2. Of those that a mesh axis runs over, the one named last changes fastest.
Arguments:
- xvals: bfloat16 [2048, 64, 640], P(('row', 'col')), may hold values from -0.3125 to 0.3125
- cols: int32 [2048, 10], replicated, may hold values from 0 to 2047, as said below
- counts: int32 [2048], replicated, may hold values from 1 to 10
Outputs:
- sign_step: float32 [2048, 64, 640], P(('row', 'col'))
Inputs may be any that keep to these rules, and one draw needn't show every extreme that they name: cols[i, 0] = i; the 10 block columns of block row i are distinct, and each is a block row held by the device that holds block row i or by one of that device's four neighbours along row or col, the ends of each axis being joined.
All inputs are finite; a program needn't handle non-finite values.
Results may differ from a plain program's by a relative error of at most 0.005.
Values may be sent and summed in bfloat16 or wider, within the bound.
A program may use at most 32 MiB of HBM per device.

v0:
```python
import jax
import jax.numpy as jnp
from jax import lax
from jax.sharding import PartitionSpec as P

ITERS = 2


def with_halo(array, sides, width):
    for axis, dim in sides:
        size, length = (lax.axis_size(axis), array.shape[dim])
        up = [(i, (i + 1) % size) for i in range(size)]
        down = [(j, i) for i, j in up]
        last = lax.slice_in_dim(array, length - width, length, axis=dim)
        leading = lax.slice_in_dim(array, 0, width, axis=dim)
        before = lax.ppermute(last, axis, up)
        after = lax.ppermute(leading, axis, down)
        array = jnp.concatenate([before, array, after], axis=dim)
    return array


def flatten_blocks(sources, block_size):
    pieces = [
        jnp.transpose(source, (0, 2, 1, 3)).reshape(-1, block_size, block_size)
        for source in sources
    ]
    pieces.append(jnp.zeros((1, block_size, block_size), jnp.bfloat16))
    return jnp.concatenate(pieces, axis=0)


def per_device(xvals, cols, counts):
    rows_here, block_size, width = xvals.shape
    slot_count = cols.shape[1]
    row_count = lax.axis_size("row")
    col_count = lax.axis_size("col")
    grid_row = lax.axis_index("row")
    grid_col = lax.axis_index("col")
    own_device = grid_row * col_count + grid_col
    first_row = own_device * rows_here
    local_cols = lax.dynamic_slice_in_dim(cols, first_row, rows_here, 0)
    local_counts = lax.dynamic_slice_in_dim(counts, first_row, rows_here, 0)
    slot_ids = jnp.arange(slot_count, dtype=jnp.int32)
    row_live = slot_ids[None, :] < local_counts[:, None]
    partner_cols = cols[local_cols]
    partner_counts = counts[local_cols]
    partner_live = slot_ids[None, None, :] < partner_counts[:, :, None]
    matches = (partner_cols[:, :, :, None] == local_cols[:, None, None, :]) & partner_live[
        :, :, :, None
    ]
    present = jnp.any(matches, axis=2)
    matched_slot = jnp.sum(matches.astype(jnp.int32) * slot_ids[None, None, :, None], axis=2)
    wanted = row_live[:, :, None] & row_live[:, None, :]
    partner_device = local_cols // rows_here
    partner_local = local_cols % rows_here
    row_step = (partner_device // col_count - grid_row) % row_count
    col_step = (partner_device % col_count - grid_col) % col_count
    partner_source = jnp.where(
        (row_step == 0) & (col_step == 0),
        0,
        jnp.where(
            row_step == row_count - 1,
            1,
            jnp.where(row_step == 1, 2, jnp.where(col_step == col_count - 1, 3, 4)),
        ),
    ).astype(jnp.int32)
    block_start = (partner_source * rows_here + partner_local) * slot_count
    lookup = jnp.where(
        present & wanted, block_start[:, :, None] + matched_slot, 5 * rows_here * slot_count
    )
    identity = jnp.eye(block_size, dtype=jnp.float32)
    diagonal_part = 3.0 * identity[:, None, :] * (slot_ids == 0).astype(jnp.float32)[None, :, None]
    current = xvals
    result = jnp.zeros((rows_here, block_size, width), jnp.float32)
    for sweep in range(ITERS):
        stored = current.reshape(rows_here, block_size, slot_count, block_size)
        neighbourhood = with_halo(current[None, None], (("row", 0), ("col", 1)), 1)
        sources = [stored] + [
            neighbourhood[spot].reshape(rows_here, block_size, slot_count, block_size)
            for spot in ((0, 1), (2, 1), (1, 0), (1, 2))
        ]
        blocks_flat = flatten_blocks(sources, block_size)

        def advance(packed, blocks_flat=blocks_flat):
            row_blocks, row_lookup = packed
            gathered = blocks_flat[row_lookup]
            square = jnp.einsum(
                "apb,pqbc->aqc", row_blocks, gathered, preferred_element_type=jnp.float32
            )
            shifted = (diagonal_part - square).astype(jnp.bfloat16)
            return 0.5 * jnp.einsum(
                "apb,pqbc->aqc", shifted, gathered, preferred_element_type=jnp.float32
            )

        result = lax.map(advance, (stored, lookup)).reshape(rows_here, block_size, width)
        current = result.astype(jnp.bfloat16)
    return result


def solution(mesh):
    return jax.shard_map(
        per_device,
        mesh=mesh,
        in_specs=(P(("row", "col"), None, None), P(), P()),
        out_specs=P(("row", "col"), None, None),
        check_vma=False,
    )
```

profile of v0, /device:TPU:6, one launch (start us, length us, event | category | flops | bytes accessed | tf_op | source)
XLA Modules:
  0.0 137.7 jit_solution(10558924388388979330)
XLA Ops:
  0.0 1.8 %copy.80 = bf16[2,64,640]{1,2,0:T(8,128)(2,1)} copy(bf16[2,64,640]{2,1,0:T(8,128)(2,1)} %param.7) | data formatting | bytes 327680 | tf_op args[0]
  1.8 4.2 %collective-permute-start = (bf16[1,1,2,64,640]{3,4,2,1,0:T(8,128)(2,1)}, bf16[1,1,2,64,640]{3,4,2,1,0:T(8,128)(2,1)S(1)}, u32[]{:S(2)}, u32[]{:S(2)}) collective-permute-start(bf16[1,1,2,64,640]{3,4,2,1,0:T(8,128)(2,1)} %bitcast.3), channel_id=1, source_target_pairs={{0,64},{64,128},{128,192},{192,256},{256,320},{320,384},{384,448},... | collective-permute-start | bytes 491528 | tf_op jit(solution)/shard_map/ppermute | solution.py:16
  6.0 1.9 %collective-permute-start.1 = (bf16[1,1,2,64,640]{3,4,2,1,0:T(8,128)(2,1)}, bf16[1,1,2,64,640]{3,4,2,1,0:T(8,128)(2,1)S(1)}, u32[]{:S(2)}, u32[]{:S(2)}) collective-permute-start(bf16[1,1,2,64,640]{3,4,2,1,0:T(8,128)(2,1)} %bitcast.3), channel_id=1, source_target_pairs={{64,0},{128,64},{192,128},{256,192},{320,256},{384,320},{448,384},... | collective-permute-start | bytes 491528 | tf_op jit(solution)/shard_map/ppermute | solution.py:17
  8.0 1.3 copy.82
  13.4 6.0 %collective-permute-done.1 = bf16[1,1,2,64,640]{3,4,2,1,0:T(8,128)(2,1)S(1)} collective-permute-done((bf16[1,1,2,64,640]{3,4,2,1,0:T(8,128)(2,1)}, bf16[1,1,2,64,640]{3,4,2,1,0:T(8,128)(2,1)S(1)}, u32[]{:S(2)}, u32[]{:S(2)}) %collective-permute-start.1) | collective-permute-done | bytes 163872 | tf_op jit(solution)/shard_map/ppermute | solution.py:17
  19.4 1.2 pad_maximum_fusion
  21.0 1.9 %collective-permute-start.2 = (bf16[3,1,2,64,640]{4,3,2,1,0:T(8,128)(2,1)S(1)}, bf16[3,1,2,64,640]{4,3,2,1,0:T(8,128)(2,1)}, u32[]{:S(2)}, u32[]{:S(2)}) collective-permute-start(bf16[3,1,2,64,640]{4,3,2,1,0:T(8,128)(2,1)S(1)} %copy.91), channel_id=1, source_target_pairs={{0,1},{1,2},{2,3},{3,4},{4,5},{5,6},{6,7},{7,8},{8,9},{9,10},{10,1... | collective-permute-start | bytes 1474568 | tf_op jit(solution)/shard_map/ppermute | solution.py:16
  22.9 18.4 %collective-permute-start.3 = (bf16[3,1,2,64,640]{4,3,2,1,0:T(8,128)(2,1)S(1)}, bf16[3,1,2,64,640]{4,3,2,1,0:T(8,128)(2,1)}, u32[]{:S(2)}, u32[]{:S(2)}) collective-permute-start(bf16[3,1,2,64,640]{4,3,2,1,0:T(8,128)(2,1)S(1)} %copy.91), channel_id=1, source_target_pairs={{1,0},{2,1},{3,2},{4,3},{5,4},{6,5},{7,6},{8,7},{9,8},{10,9},{11,1... | collective-permute-start | bytes 1474568 | tf_op jit(solution)/shard_map/ppermute | solution.py:17
  41.4 1.2 copy.95
  43.2 3.2 %collective-permute-done.2 = bf16[3,1,2,64,640]{4,3,2,1,0:T(8,128)(2,1)} collective-permute-done((bf16[3,1,2,64,640]{4,3,2,1,0:T(8,128)(2,1)S(1)}, bf16[3,1,2,64,640]{4,3,2,1,0:T(8,128)(2,1)}, u32[]{:S(2)}, u32[]{:S(2)}) %collective-permute-start.2) | collective-permute-done | bytes 491552 | tf_op jit(solution)/shard_map/ppermute | solution.py:16
  46.4 0.9 slice.24
  47.7 16.0 %collective-permute-done.3 = bf16[3,1,2,64,640]{4,3,2,1,0:T(8,128)(2,1)} collective-permute-done((bf16[3,1,2,64,640]{4,3,2,1,0:T(8,128)(2,1)S(1)}, bf16[3,1,2,64,640]{4,3,2,1,0:T(8,128)(2,1)}, u32[]{:S(2)}, u32[]{:S(2)}) %collective-permute-start.3) | collective-permute-done | bytes 491552 | tf_op jit(solution)/shard_map/ppermute | solution.py:17
  65.2 7.0 %while.22 = (s32[]{:T(128)}, bf16[2,64,10,64]{3,1,2,0:T(8,128)(2,1)}, bf16[2,64,10,64]{1,3,2,0:T(8,128)(2,1)}, s32[2,10,10]{2,0,1:T(2,128)S(1)}, bf16[101,64,64]...) while((s32[]{:T(128)}, bf16[2,64,10,64]{3,1,2,0:T(8,128)(2,1)}, ...), condition=%wide.region_3.4_spmd.clone, body=%wide.region_2.3_spmd.clone.sunk | while | flops 105022768 | bytes 5283769 | solution.py:94
  66.2 2.5 %fusion.66 = bf16[2,64,10,64]{3,1,2,0:T(8,128)(2,1)} fusion(bf16[2,64,10,64]{3,1,2,0:T(8,128)(2,1)} %get-tuple-element.260, s32[]{:T(128)} %get-tuple-element.259, bf16[10,10,64,64]{3,2,1,0:T(8,128)(2,1)S(1)} %bitcast.176, f32[10]{0:T(128)S(1)} %get-tuple-element.272, f32[64,64]{1,0:T(8,128)S(1)} %get-tuple-element.273, ...), kind=kOutput, calls=%fused_computation.9.clone.1 | convolution fusion | flops 105021440 | bytes 3638784 | tf_op jit(solution)/shard_map/while/body/eval_jaxpr/apb,pqbc->aqc/dot_general | solution.py:90
  69.7 2.5 %fusion.66 = bf16[2,64,10,64]{3,1,2,0:T(8,128)(2,1)} fusion(bf16[2,64,10,64]{3,1,2,0:T(8,128)(2,1)} %get-tuple-element.260, s32[]{:T(128)} %get-tuple-element.259, bf16[10,10,64,64]{3,2,1,0:T(8,128)(2,1)S(1)} %bitcast.176, f32[10]{0:T(128)S(1)} %get-tuple-element.272, f32[64,64]{1,0:T(8,128)S(1)} %get-tuple-element.273, ...), kind=kOutput, calls=%fused_computation.9.clone.1 | convolution fusion | flops 105021440 | bytes 3638784 | tf_op jit(solution)/shard_map/while/body/eval_jaxpr/apb,pqbc->aqc/dot_general | solution.py:90
  72.1 1.2 copy.102
  73.3 1.9 %collective-permute-start.4 = (bf16[1,1,2,64,640]{3,4,2,1,0:T(8,128)(2,1)S(1)}, bf16[1,1,2,64,640]{3,4,2,1,0:T(8,128)(2,1)S(1)}, u32[]{:S(2)}, u32[]{:S(2)}) collective-permute-start(bf16[1,1,2,64,640]{3,4,2,1,0:T(8,128)(2,1)S(1)} %bitcast.186), channel_id=1, source_target_pairs={{0,64},{64,128},{128,192},{192,256},{256,320},{320,384},{384,448},... | collective-permute-start | bytes 491528 | tf_op jit(solution)/shard_map/ppermute | solution.py:16
  75.2 3.9 %collective-permute-start.5 = (bf16[1,1,2,64,640]{3,4,2,1,0:T(8,128)(2,1)S(1)}, bf16[1,1,2,64,640]{3,4,2,1,0:T(8,128)(2,1)S(1)}, u32[]{:S(2)}, u32[]{:S(2)}) collective-permute-start(bf16[1,1,2,64,640]{3,4,2,1,0:T(8,128)(2,1)S(1)} %bitcast.187), channel_id=1, source_target_pairs={{64,0},{128,64},{192,128},{256,192},{320,256},{384,320},{448,384},... | collective-permute-start | bytes 491528 | tf_op jit(solution)/shard_map/ppermute | solution.py:17
  79.2 3.1 %collective-permute-done.4 = bf16[1,1,2,64,640]{3,4,2,1,0:T(8,128)(2,1)S(1)} collective-permute-done((bf16[1,1,2,64,640]{3,4,2,1,0:T(8,128)(2,1)S(1)}, bf16[1,1,2,64,640]{3,4,2,1,0:T(8,128)(2,1)S(1)}, u32[]{:S(2)}, u32[]{:S(2)}) %collective-permute-start.4) | collective-permute-done | bytes 163872 | tf_op jit(solution)/shard_map/ppermute | solution.py:16
  82.3 4.0 %collective-permute-done.5 = bf16[1,1,2,64,640]{3,4,2,1,0:T(8,128)(2,1)S(1)} collective-permute-done((bf16[1,1,2,64,640]{3,4,2,1,0:T(8,128)(2,1)S(1)}, bf16[1,1,2,64,640]{3,4,2,1,0:T(8,128)(2,1)S(1)}, u32[]{:S(2)}, u32[]{:S(2)}) %collective-permute-start.5) | collective-permute-done | bytes 163872 | tf_op jit(solution)/shard_map/ppermute | solution.py:17
  86.9 1.9 %collective-permute-start.6 = (bf16[3,1,2,64,640]{4,3,2,1,0:T(8,128)(2,1)S(1)}, bf16[3,1,2,64,640]{4,3,2,1,0:T(8,128)(2,1)}, u32[]{:S(2)}, u32[]{:S(2)}) collective-permute-start(bf16[3,1,2,64,640]{4,3,2,1,0:T(8,128)(2,1)S(1)} %copy.103), channel_id=1, source_target_pairs={{0,1},{1,2},{2,3},{3,4},{4,5},{5,6},{6,7},{7,8},{8,9},{9,10},{10,1... | collective-permute-start | bytes 1474568 | tf_op jit(solution)/shard_map/ppermute | solution.py:16
  88.9 12.5 %collective-permute-start.7 = (bf16[3,1,2,64,640]{4,3,2,1,0:T(8,128)(2,1)S(1)}, bf16[3,1,2,64,640]{4,3,2,1,0:T(8,128)(2,1)}, u32[]{:S(2)}, u32[]{:S(2)}) collective-permute-start(bf16[3,1,2,64,640]{4,3,2,1,0:T(8,128)(2,1)S(1)} %copy.103), channel_id=1, source_target_pairs={{1,0},{2,1},{3,2},{4,3},{5,4},{6,5},{7,6},{8,7},{9,8},{10,9},{11,1... | collective-permute-start | bytes 1474568 | tf_op jit(solution)/shard_map/ppermute | solution.py:17
  101.4 1.0 constant_dynamic-update-slice_fusion.12
  102.9 19.0 %collective-permute-done.6 = bf16[3,1,2,64,640]{4,3,2,1,0:T(8,128)(2,1)} collective-permute-done((bf16[3,1,2,64,640]{4,3,2,1,0:T(8,128)(2,1)S(1)}, bf16[3,1,2,64,640]{4,3,2,1,0:T(8,128)(2,1)}, u32[]{:S(2)}, u32[]{:S(2)}) %collective-permute-start.6) | collective-permute-done | bytes 491552 | tf_op jit(solution)/shard_map/ppermute | solution.py:16
  121.9 0.9 slice.26
  123.3 0.9 slice.27
  124.8 10.9 %while.23 = (s32[]{:T(128)}, f32[2,64,10,64]{1,3,2,0:T(8,128)}, bf16[2,64,10,64]{3,1,2,0:T(8,128)(2,1)}, s32[2,10,10]{2,0,1:T(2,128)S(1)}, bf16[101,64,64]{2,1,0...) while((s32[]{:T(128)}, f32[2,64,10,64]{1,3,2,0:T(8,128)}, ...), condition=%wide.region_5.6_spmd.clone, body=%wide.region_4.5_spmd.clone.sunk | while | flops 105022768 | bytes 6102969 | solution.py:94
  125.8 2.6 %fusion.71 = f32[1,64,10,64]{3,1,2,0:T(8,128)} fusion(bf16[10,10,64,64]{3,2,1,0:T(8,128)(2,1)S(1)} %bitcast.177, f32[10]{0:T(128)S(1)} %get-tuple-element.296, f32[64,64]{1,0:T(8,128)S(1)} %get-tuple-element.297, bf16[2,64,10,64]{3,1,2,0:T(8,128)(2,1)} %get-tuple-element.293, s32[]{:T(128)} %get-tuple-element.283), kind=kOutput, calls=%fused_computation.25.clone.1 | convolution fusion | flops 105021440 | bytes 3638272 | tf_op jit(solution)/shard_map/while/body/eval_jaxpr/apb,pqbc->aqc/dot_general | solution.py:90
  128.4 1.1 copy.135
  131.2 2.5 %fusion.71 = f32[1,64,10,64]{3,1,2,0:T(8,128)} fusion(bf16[10,10,64,64]{3,2,1,0:T(8,128)(2,1)S(1)} %bitcast.177, f32[10]{0:T(128)S(1)} %get-tuple-element.296, f32[64,64]{1,0:T(8,128)S(1)} %get-tuple-element.297, bf16[2,64,10,64]{3,1,2,0:T(8,128)(2,1)} %get-tuple-element.293, s32[]{:T(128)} %get-tuple-element.283), kind=kOutput, calls=%fused_computation.25.clone.1 | convolution fusion | flops 105021440 | bytes 3638272 | tf_op jit(solution)/shard_map/while/body/eval_jaxpr/apb,pqbc->aqc/dot_general | solution.py:90
  133.8 1.1 copy.135
  135.7 2.0 %copy.113 = f32[2,64,640]{2,1,0:T(8,128)} copy(f32[2,64,640]{1,2,0:T(8,128)} %bitcast.189) | data formatting | bytes 655360 | tf_op jit(solution)/shard_map/reshape | solution.py:94
  (73 shorter events, 14.4 us)
Async XLA Ops:
  0.0 11.1 %copy-start = (s32[2048]{0:T(1024)S(1)}, s32[2048]{0:T(1024)}, u32[]{:S(2)}) copy-start(s32[2048]{0:T(1024)} %param.9) | copy-start | bytes 24580
  1.8 11.5 %collective-permute-start = (bf16[1,1,2,64,640]{3,4,2,1,0:T(8,128)(2,1)}, bf16[1,1,2,64,640]{3,4,2,1,0:T(8,128)(2,1)S(1)}, u32[]{:S(2)}, u32[]{:S(2)}) collective-permute-start(bf16[1,1,2,64,640]{3,4,2,1,0:T(8,128)(2,1)} %bitcast.3), channel_id=1, source_target_pairs={{0,64},{64,128},{128,192},{192,256},{256,320},{320,384},{384,448},... | collective-permute-start | bytes 491528 | tf_op jit(solution)/shard_map/ppermute | solution.py:16
  6.0 13.4 %collective-permute-start.1 = (bf16[1,1,2,64,640]{3,4,2,1,0:T(8,128)(2,1)}, bf16[1,1,2,64,640]{3,4,2,1,0:T(8,128)(2,1)S(1)}, u32[]{:S(2)}, u32[]{:S(2)}) collective-permute-start(bf16[1,1,2,64,640]{3,4,2,1,0:T(8,128)(2,1)} %bitcast.3), channel_id=1, source_target_pairs={{64,0},{128,64},{192,128},{256,192},{320,256},{384,320},{448,384},... | collective-permute-start | bytes 491528 | tf_op jit(solution)/shard_map/ppermute | solution.py:17
  21.0 25.4 %collective-permute-start.2 = (bf16[3,1,2,64,640]{4,3,2,1,0:T(8,128)(2,1)S(1)}, bf16[3,1,2,64,640]{4,3,2,1,0:T(8,128)(2,1)}, u32[]{:S(2)}, u32[]{:S(2)}) collective-permute-start(bf16[3,1,2,64,640]{4,3,2,1,0:T(8,128)(2,1)S(1)} %copy.91), channel_id=1, source_target_pairs={{0,1},{1,2},{2,3},{3,4},{4,5},{5,6},{6,7},{7,8},{8,9},{9,10},{10,1... | collective-permute-start | bytes 1474568 | tf_op jit(solution)/shard_map/ppermute | solution.py:16
  22.9 40.7 %collective-permute-start.3 = (bf16[3,1,2,64,640]{4,3,2,1,0:T(8,128)(2,1)S(1)}, bf16[3,1,2,64,640]{4,3,2,1,0:T(8,128)(2,1)}, u32[]{:S(2)}, u32[]{:S(2)}) collective-permute-start(bf16[3,1,2,64,640]{4,3,2,1,0:T(8,128)(2,1)S(1)} %copy.91), channel_id=1, source_target_pairs={{1,0},{2,1},{3,2},{4,3},{5,4},{6,5},{7,6},{8,7},{9,8},{10,9},{11,1... | collective-permute-start | bytes 1474568 | tf_op jit(solution)/shard_map/ppermute | solution.py:17
  73.3 9.0 %collective-permute-start.4 = (bf16[1,1,2,64,640]{3,4,2,1,0:T(8,128)(2,1)S(1)}, bf16[1,1,2,64,640]{3,4,2,1,0:T(8,128)(2,1)S(1)}, u32[]{:S(2)}, u32[]{:S(2)}) collective-permute-start(bf16[1,1,2,64,640]{3,4,2,1,0:T(8,128)(2,1)S(1)} %bitcast.186), channel_id=1, source_target_pairs={{0,64},{64,128},{128,192},{192,256},{256,320},{320,384},{384,448},... | collective-permute-start | bytes 491528 | tf_op jit(solution)/shard_map/ppermute | solution.py:16
  75.2 11.1 %collective-permute-start.5 = (bf16[1,1,2,64,640]{3,4,2,1,0:T(8,128)(2,1)S(1)}, bf16[1,1,2,64,640]{3,4,2,1,0:T(8,128)(2,1)S(1)}, u32[]{:S(2)}, u32[]{:S(2)}) collective-permute-start(bf16[1,1,2,64,640]{3,4,2,1,0:T(8,128)(2,1)S(1)} %bitcast.187), channel_id=1, source_target_pairs={{64,0},{128,64},{192,128},{256,192},{320,256},{384,320},{448,384},... | collective-permute-start | bytes 491528 | tf_op jit(solution)/shard_map/ppermute | solution.py:17
  86.9 35.0 %collective-permute-start.6 = (bf16[3,1,2,64,640]{4,3,2,1,0:T(8,128)(2,1)S(1)}, bf16[3,1,2,64,640]{4,3,2,1,0:T(8,128)(2,1)}, u32[]{:S(2)}, u32[]{:S(2)}) collective-permute-start(bf16[3,1,2,64,640]{4,3,2,1,0:T(8,128)(2,1)S(1)} %copy.103), channel_id=1, source_target_pairs={{0,1},{1,2},{2,3},{3,4},{4,5},{5,6},{6,7},{7,8},{8,9},{9,10},{10,1... | collective-permute-start | bytes 1474568 | tf_op jit(solution)/shard_map/ppermute | solution.py:16
  88.9 34.4 %collective-permute-start.7 = (bf16[3,1,2,64,640]{4,3,2,1,0:T(8,128)(2,1)S(1)}, bf16[3,1,2,64,640]{4,3,2,1,0:T(8,128)(2,1)}, u32[]{:S(2)}, u32[]{:S(2)}) collective-permute-start(bf16[3,1,2,64,640]{4,3,2,1,0:T(8,128)(2,1)S(1)} %copy.103), channel_id=1, source_target_pairs={{1,0},{2,1},{3,2},{4,3},{5,4},{6,5},{7,6},{8,7},{9,8},{10,9},{11,1... | collective-permute-start | bytes 1474568 | tf_op jit(solution)/shard_map/ppermute | solution.py:17
where the time goes:
time: 139 us; the launch traced here: 138 us
  waiting for transfers between devices  51.9 us (37%)
  starting transfers between devices  46.8 us (34%)
  local copies, waits for them, and re-layouts  25.4 us (18%)
  matrix products  10.1 us (7%)
  other arithmetic  3.16 us (2%)
    ppermute x4, starting transfers between devices, with_halo(): after = lax.ppermute(leading, axis, down)  36.8 us
    ppermute x4, waiting for transfers between devices, with_halo(): after = lax.ppermute(leading, axis, down)  26 us
    ppermute x4, waiting for transfers between devices, with_halo(): before = lax.ppermute(last, axis, up)  25.8 us
    dot_general x4, matrix products, advance(): jnp.einsum('apb,pqbc->aqc', shifted, gathered, preferred_element_type=jnp...  10.1 us
    ppermute x4, starting transfers between devices, with_halo(): before = lax.ppermute(last, axis, up)  9.95 us
    unnamed x19, local copies, waits for them, and re-layouts  5.35 us
    dynamic_update_slice x4, local copies, waits for them, and re-layouts, per_device(): lax.map(advance, (stored, lookup)).reshape(rows_here, block_size, width)  3.74 us
    slice x4, local copies, waits for them, and re-layouts, per_device(): neighbourhood[spot].reshape(rows_here, block_size, slot_count, block_size)  3.72 us
  transfers between devices with their start and end apart: 8, of which 7 were waited for; matrix products, arithmetic and copies ran while one was open for 8% of the time, Pallas kernels for 0%

commit v1 on v0

v1 whole, which is shorter than its diff:
```python
import functools

import jax
import jax.numpy as jnp
from jax import lax
from jax.experimental import pallas as pl
from jax.experimental.pallas import tpu as pltpu
from jax.sharding import PartitionSpec as P

MESH = pl.DeviceIdType.MESH
F32 = jnp.float32
BF16 = jnp.bfloat16


def dot(a, b):
    return jnp.dot(a, b, preferred_element_type=F32)


def kernel(
    row_count, col_count, block, slots,
    x_hbm, cols_hbm, counts_hbm, out_hbm,
    xs, tiles, cnts, can, toward, diag, s0, s0_in, y0, y0_in, outv,
    local_sem, send_sem, recv_sem,
):
    pair = 2 * block
    r = lax.axis_index("row")
    c = lax.axis_index("col")
    up, down = lax.rem(r + row_count - 1, row_count), lax.rem(r + 1, row_count)
    left, right = lax.rem(c + col_count - 1, col_count), lax.rem(c + 1, col_count)
    places = [(up, c), (down, c), (r, left), (r, right)]

    barrier = pltpu.get_barrier_semaphore()
    for place in places:
        pl.semaphore_signal(barrier, inc=1, device_id=place, device_id_type=MESH)

    width = 2 * col_count
    loads = []
    for at, grid_row in enumerate((r, up, down)):
        lanes = pl.ds(pl.multiple_of(grid_row * width, width), width)
        loads.append(
            pltpu.make_async_copy(cols_hbm.at[:, lanes], tiles.at[at], local_sem.at[at])
        )
    loads.append(pltpu.make_async_copy(counts_hbm, cnts, local_sem.at[3]))
    loads.append(pltpu.make_async_copy(x_hbm, xs, local_sem.at[4]))
    for load in loads:
        load.start()

    lane = lax.broadcasted_iota(jnp.int32, (1, pair), 1)
    second = (lane >= block).astype(jnp.int32)
    tile_lane = lax.broadcasted_iota(jnp.int32, (1, width), 1)
    slot_id = lax.broadcasted_iota(jnp.int32, (slots, 1), 0).astype(F32)
    devices = [r * col_count + c] + [a * col_count + b for a, b in places]
    wide = [(2 * device + second).astype(F32) for device in devices]

    def stored_row(at, grid_row, grid_col, which):
        here = tile_lane == 2 * grid_col + which
        ids = jnp.sum(jnp.where(here, tiles[at].astype(F32), 0.0), axis=1, keepdims=True)
        count_row = cnts[pl.ds(grid_row, 1), :].astype(F32)
        count = jnp.sum(jnp.where(here, count_row, 0.0), axis=1, keepdims=True)
        return jnp.where(slot_id < count, ids, -1.0)

    for load in loads[:4]:
        load.wait()
    own = [stored_row(0, r, c, which) for which in range(2)]
    masks = [[(own[i] == wide[g]) for g in range(5)] for i in range(2)]

    def live(parts):
        return jnp.concatenate(
            [
                jnp.broadcast_to(
                    jnp.max(part.astype(F32), axis=0, keepdims=True), (block, pair)
                )
                for part in parts
            ],
            axis=0,
        )

    first_half = lane < block
    loads[4].wait()
    for i in range(2):
        sums = [jnp.zeros((block, pair), F32) for _ in range(5)]
        for j in range(slots // 2):
            both = xs[i, :, j * pair : (j + 1) * pair].astype(F32)
            turned = pltpu.roll(both, block, 1)
            for slot, doubled in (
                (2 * j, jnp.where(first_half, both, turned)),
                (2 * j + 1, jnp.where(first_half, turned, both)),
            ):
                for g in range(5):
                    sums[g] = jnp.where(masks[i][g][slot : slot + 1], doubled, sums[g])
        for g in range(5):
            can[g, i * block : (i + 1) * block, :] = sums[g].astype(BF16)

    pl.semaphore_wait(barrier, 4)
    order = (2, 3, 0, 1)

    def send(src, dst, kind, e):
        copy = pltpu.make_async_remote_copy(
            src_ref=src,
            dst_ref=dst.at[e ^ 1],
            send_sem=send_sem.at[kind, e],
            recv_sem=recv_sem.at[kind, e ^ 1],
            device_id=places[e],
            device_id_type=MESH,
        )
        copy.start()
        return copy

    def arrival(dst, kind, e):
        return pltpu.make_async_remote_copy(
            src_ref=dst.at[e],
            dst_ref=dst.at[e],
            send_sem=send_sem.at[kind, e],
            recv_sem=recv_sem.at[kind, e],
            device_id=places[e],
            device_id_type=MESH,
        )

    sent = [send(can.at[e + 1], toward, 0, e) for e in order]
    sent += [send(can.at[0], diag, 1, e) for e in order]

    own_live = [live([masks[i][g] for i in range(2)]) for g in range(5)]
    near_live = []
    for e, (at, (grid_row, grid_col)) in enumerate(zip((1, 2, 0, 0), places)):
        rows = [stored_row(at, grid_row, grid_col, which) for which in range(2)]
        near_live.append(live([row == wide[0] for row in rows]))
    x0 = can[0]
    xe = [can[e + 1] for e in range(4)]
    square = dot(x0, x0)
    x0_xe = [dot(x0, xe[e]) for e in range(4)]
    eye = lax.broadcasted_iota(jnp.int32, (pair, pair), 0) == lax.broadcasted_iota(
        jnp.int32, (pair, pair), 1
    )
    three = jnp.where(eye, 3.0, 0.0)

    for e in order:
        arrival(toward, 0, e).wait_recv()
        square += dot(xe[e], toward[e])
    s0[...] = (three - square * own_live[0]).astype(BF16)
    sent += [send(s0, s0_in, 2, e) for e in order]

    near_s = [dot(toward[e], x0) for e in range(4)]
    following = dot(s0[...], x0)
    side_s = [None] * 4
    for e in order:
        arrival(diag, 1, e).wait_recv()
        side = x0_xe[e] + dot(xe[e], diag[e])
        side_s[e] = (-side * own_live[e + 1]).astype(BF16)
        following += dot(side_s[e], toward[e])
    y0[...] = (0.5 * following * own_live[0]).astype(BF16)
    sent += [send(y0, y0_in, 3, e) for e in order]

    ye = []
    near_part = []
    for e in range(4):
        side = dot(s0[...], xe[e]) + dot(side_s[e], diag[e])
        ye.append((0.5 * side * own_live[e + 1]).astype(BF16))
        near = near_s[e] + dot(diag[e], toward[e])
        near = (-near * near_live[e]).astype(BF16)
        near_part.append(dot(near, x0))
    square = dot(y0[...], y0[...])
    y0_ye = [dot(y0[...], ye[e]) for e in range(4)]
    near_y = [None] * 4
    for e in order:
        arrival(s0_in, 2, e).wait_recv()
        near = near_part[e] + dot(s0_in[e], toward[e])
        near_y[e] = (0.5 * near * near_live[e]).astype(BF16)
        square += dot(ye[e], near_y[e])
    last_s = (three - square * own_live[0]).astype(BF16)
    results = [dot(last_s, y0[...])] + [dot(last_s, ye[e]) for e in range(4)]
    for e in order:
        arrival(y0_in, 3, e).wait_recv()
        side = y0_ye[e] + dot(ye[e], y0_in[e])
        side = (-side * own_live[e + 1]).astype(BF16)
        results[0] += dot(side, near_y[e])
        results[e + 1] += dot(side, y0_in[e])

    stores = []
    place_id = lax.broadcasted_iota(jnp.int32, (slots, 1), 0)
    holder = jnp.zeros((slots, 1), jnp.int32)
    for g in range(5):
        holder = jnp.where(place_id // 2 == g, devices[g], holder)
    candidate = (2 * holder + place_id % 2).astype(F32)
    for i in range(2):
        chosen = []
        for j in range(slots // 2):
            names = jnp.where(first_half, own[i][2 * j : 2 * j + 1], own[i][2 * j + 1 : 2 * j + 2])
            chosen.append(candidate == names)
        sums = [jnp.zeros((block, pair), F32) for _ in range(5)]
        for g in range(5):
            both = 0.5 * results[g][i * block : (i + 1) * block, :]
            turned = pltpu.roll(both, block, 1)
            for spot, doubled in (
                (2 * g, jnp.where(first_half, both, turned)),
                (2 * g + 1, jnp.where(first_half, turned, both)),
            ):
                for j in range(slots // 2):
                    sums[j] = jnp.where(chosen[j][spot : spot + 1], doubled, sums[j])
        for j in range(slots // 2):
            outv[i, :, j * pair : (j + 1) * pair] = sums[j]
        store = pltpu.make_async_copy(outv.at[i], out_hbm.at[i], local_sem.at[5 + i])
        store.start()
        stores.append(store)
    for copy in sent:
        copy.wait_send()
    for store in stores:
        store.wait()


def per_device(xvals, cols, counts):
    rows_here, block, _ = xvals.shape
    slots = cols.shape[1]
    row_count = lax.axis_size("row")
    col_count = lax.axis_size("col")
    width = rows_here * col_count
    pair = 2 * block
    square = (pair, pair)
    any_space = pl.BlockSpec(memory_space=pl.ANY)
    return pl.pallas_call(
        functools.partial(kernel, row_count, col_count, block, slots),
        out_shape=jax.ShapeDtypeStruct(xvals.shape, F32),
        in_specs=[any_space] * 3,
        out_specs=any_space,
        scratch_shapes=[
            pltpu.VMEM(xvals.shape, BF16),
            pltpu.VMEM((3, slots, width), jnp.int32),
            pltpu.VMEM((row_count, width), jnp.int32),
            pltpu.VMEM((5,) + square, BF16),
            pltpu.VMEM((4,) + square, BF16),
            pltpu.VMEM((4,) + square, BF16),
            pltpu.VMEM(square, BF16),
            pltpu.VMEM((4,) + square, BF16),
            pltpu.VMEM(square, BF16),
            pltpu.VMEM((4,) + square, BF16),
            pltpu.VMEM(xvals.shape, F32),
            pltpu.SemaphoreType.DMA((7,)),
            pltpu.SemaphoreType.DMA((4, 4)),
            pltpu.SemaphoreType.DMA((4, 4)),
        ],
        compiler_params=pltpu.CompilerParams(
            collective_id=0, has_side_effects=True, vmem_limit_bytes=60 * 1024 * 1024
        ),
        cost_estimate=pl.CostEstimate(
            flops=250_000_000, bytes_accessed=600_000, transcendentals=0
        ),
        name="sign_steps",
    )(xvals, cols.T, counts.reshape(row_count, width))


def solution(mesh):
    return jax.shard_map(
        per_device,
        mesh=mesh,
        in_specs=(P(("row", "col"), None, None), P(), P()),
        out_specs=P(("row", "col"), None, None),
        check_vma=False,
    )
```

time: 139 us -> 38.3 us (0.28)
  the two profiles are of different devices: /device:TPU:6 before, /device:TPU:64 now
where the time goes in v1:
time: 38.3 us; the launch traced here: 38.1 us
  Pallas kernels  36.4 us (95%)
  local copies, waits for them, and re-layouts  1.72 us (4%)
    pallas_call x1, Pallas kernels, per_device(): pl.pallas_call(functools.partial(kernel, row_count, col_count, block, slo...  36.4 us
    unnamed x1, local copies, waits for them, and re-layouts  1.72 us

profile of v1, /device:TPU:64, one launch (start us, length us, event | category | flops | bytes accessed | tf_op | source)
XLA Modules:
  0.0 38.1 jit_solution(13090860832151811865)
XLA Ops:
  0.0 36.4 %sign_steps.1 = f32[2,64,640]{2,1,0:T(8,128)} custom-call(bf16[2,64,640]{2,1,0:T(8,128)(2,1)} %x_hbm.1, s32[10,2048]{1,0:T(8,128)} %bitcast.2, s32[16,128]{1,0:T(8,128)} %bitcast.3), custom_call_target="tpu_custom_call" | custom-call | flops 250000000 | bytes 600000 | tf_op jit(solution)/shard_map/sign_steps/pallas_call | solution.py:219
  36.4 1.7 %copy.5 = f32[2,64,640]{2,1,0:T(8,128)} copy(f32[2,64,640]{2,1,0:T(8,128)} %sign_steps.1) | data formatting | bytes 655360

commit v2 on v1

--- a/solution.py
+++ b/solution.py
@@ -19,19 +19,33 @@
 def kernel(
     row_count, col_count, block, slots,
     x_hbm, cols_hbm, counts_hbm, out_hbm,
-    xs, tiles, cnts, can, toward, diag, s0, s0_in, y0, y0_in, outv,
-    local_sem, send_sem, recv_sem,
+    xs, tiles, cnts, can, toward, diag, s0, s0_in, y0, y0_in, part_a, part_b, outv,
+    local_sem, send_sem, recv_sem, hello,
 ):
     pair = 2 * block
     r = lax.axis_index("row")
     c = lax.axis_index("col")
     up, down = lax.rem(r + row_count - 1, row_count), lax.rem(r + 1, row_count)
-    left, right = lax.rem(c + col_count - 1, col_count), lax.rem(c + 1, col_count)
-    places = [(up, c), (down, c), (r, left), (r, right)]
-
+    odd = lax.rem(c, 2)
+    beside = c + 1 - 2 * odd
+    beyond = lax.rem(c + col_count - 1 + 2 * odd, col_count)
+    places = [(up, c), (down, c), (r, beside), (r, beyond)]
+    back = (1, 0, 2, 3)
+    near, far = (0, 1, 2), 3
+
+    def rank(row, col):
+        z = lax.rem(lax.div(col, 2), 4) * 4 + lax.div(row, 4)
+        usual = (z * 64 + lax.div(col, 8)) * 8 + lax.rem(row, 4) * 2 + lax.rem(col, 2)
+        return jnp.where(row + col == 0, 12 * 512 - 1, usual)
+
+    mine = rank(r, c)
+    later = [rank(*place) > mine for place in places]
     barrier = pltpu.get_barrier_semaphore()
-    for place in places:
-        pl.semaphore_signal(barrier, inc=1, device_id=place, device_id_type=MESH)
+    for e in range(4):
+
+        @pl.when(later[e])
+        def _(e=e):
+            pl.semaphore_signal(barrier, inc=1, device_id=places[e], device_id_type=MESH)
 
     width = 2 * col_count
     loads = []
@@ -44,6 +58,20 @@
     loads.append(pltpu.make_async_copy(x_hbm, xs, local_sem.at[4]))
     for load in loads:
         load.start()
+
+    earlier = sum(1 - late.astype(jnp.int32) for late in later)
+
+    @pl.when(earlier > 0)
+    def _():
+        pl.semaphore_wait(barrier, earlier)
+
+    for e in range(4):
+
+        @pl.when(jnp.logical_not(later[e]))
+        def _(e=e):
+            pl.semaphore_signal(
+                hello.at[back[e]], inc=1, device_id=places[e], device_id_type=MESH
+            )
 
     lane = lax.broadcasted_iota(jnp.int32, (1, pair), 1)
     second = (lane >= block).astype(jnp.int32)
@@ -91,19 +119,18 @@
         for g in range(5):
             can[g, i * block : (i + 1) * block, :] = sums[g].astype(BF16)
 
-    pl.semaphore_wait(barrier, 4)
-    order = (2, 3, 0, 1)
-
-    def send(src, dst, kind, e):
+    sent = []
+
+    def post(src, dst, kind, e):
         copy = pltpu.make_async_remote_copy(
             src_ref=src,
-            dst_ref=dst.at[e ^ 1],
+            dst_ref=dst.at[back[e]],
             send_sem=send_sem.at[kind, e],
-            recv_sem=recv_sem.at[kind, e ^ 1],
+            recv_sem=recv_sem.at[kind, back[e]],
             device_id=places[e],
             device_id_type=MESH,
         )
-        copy.start()
+        sent.append(copy)
         return copy
 
     def arrival(dst, kind, e):
@@ -116,14 +143,33 @@
             device_id_type=MESH,
         )
 
-    sent = [send(can.at[e + 1], toward, 0, e) for e in order]
-    sent += [send(can.at[0], diag, 1, e) for e in order]
+    first = [
+        [post(can.at[e + 1], toward, 0, e), post(can.at[0], diag, 1, e)] for e in range(4)
+    ]
+    sums_a = post(part_a, s0_in, 2, far)
+    sums_b = post(part_b, y0_in, 3, far)
+
+    @pl.when(jnp.logical_not(later[far]))
+    def _():
+        for copy in first[far]:
+            copy.start()
+
+    for e in near:
+
+        @pl.when(later[e])
+        def _(e=e):
+            pl.semaphore_wait(hello.at[e], 1)
+
+        for copy in first[e]:
+            copy.start()
 
     own_live = [live([masks[i][g] for i in range(2)]) for g in range(5)]
     near_live = []
     for e, (at, (grid_row, grid_col)) in enumerate(zip((1, 2, 0, 0), places)):
         rows = [stored_row(at, grid_row, grid_col, which) for which in range(2)]
         near_live.append(live([row == wide[0] for row in rows]))
+        if e == far:
+            far_live = live([row == wide[far + 1] for row in rows])
     x0 = can[0]
     xe = [can[e + 1] for e in range(4)]
     square = dot(x0, x0)
@@ -133,47 +179,84 @@
     )
     three = jnp.where(eye, 3.0, 0.0)
 
-    for e in order:
+    for e in near:
         arrival(toward, 0, e).wait_recv()
         square += dot(xe[e], toward[e])
-    s0[...] = (three - square * own_live[0]).astype(BF16)
-    sent += [send(s0, s0_in, 2, e) for e in order]
-
-    near_s = [dot(toward[e], x0) for e in range(4)]
-    following = dot(s0[...], x0)
+    part_a[...] = square.astype(BF16)
+
+    @pl.when(jnp.logical_not(later[far]))
+    def _():
+        sums_a.start()
+
     side_s = [None] * 4
-    for e in order:
+    following = jnp.zeros((pair, pair), F32)
+    for e in near:
         arrival(diag, 1, e).wait_recv()
         side = x0_xe[e] + dot(xe[e], diag[e])
         side_s[e] = (-side * own_live[e + 1]).astype(BF16)
         following += dot(side_s[e], toward[e])
-    y0[...] = (0.5 * following * own_live[0]).astype(BF16)
-    sent += [send(y0, y0_in, 3, e) for e in order]
+    part_b[...] = following.astype(BF16)
+
+    @pl.when(jnp.logical_not(later[far]))
+    def _():
+        sums_b.start()
+
+    @pl.when(later[far])
+    def _():
+        pl.semaphore_wait(hello.at[far], 1)
+        for copy in first[far] + [sums_a, sums_b]:
+            copy.start()
+
+
+    arrival(toward, 0, far).wait_recv()
+    square += dot(xe[far], toward[far])
+    s0[...] = (three - square * own_live[0]).astype(BF16)
+    for e in near:
+        post(s0, s0_in, 2, e).start()
+    added = dot(s0[...], x0)
+    arrival(diag, 1, far).wait_recv()
+    side = x0_xe[far] + dot(xe[far], diag[far])
+    side_s[far] = (-side * own_live[far + 1]).astype(BF16)
+    added += dot(side_s[far], toward[far])
+    y0[...] = (0.5 * (following + added) * own_live[0]).astype(BF16)
+    for e in near:
+        post(y0, y0_in, 3, e).start()
 
     ye = []
     near_part = []
     for e in range(4):
         side = dot(s0[...], xe[e]) + dot(side_s[e], diag[e])
         ye.append((0.5 * side * own_live[e + 1]).astype(BF16))
-        near = near_s[e] + dot(diag[e], toward[e])
-        near = (-near * near_live[e]).astype(BF16)
-        near_part.append(dot(near, x0))
+        theirs = dot(toward[e], x0) + dot(diag[e], toward[e])
+        theirs = (-theirs * near_live[e]).astype(BF16)
+        near_part.append(dot(theirs, x0))
+    far_square = dot(toward[far], xe[far])
+    far_following = dot(theirs, xe[far])
     square = dot(y0[...], y0[...])
     y0_ye = [dot(y0[...], ye[e]) for e in range(4)]
     near_y = [None] * 4
-    for e in order:
+    for e in near:
         arrival(s0_in, 2, e).wait_recv()
-        near = near_part[e] + dot(s0_in[e], toward[e])
-        near_y[e] = (0.5 * near * near_live[e]).astype(BF16)
+        theirs = near_part[e] + dot(s0_in[e], toward[e])
+        near_y[e] = (0.5 * theirs * near_live[e]).astype(BF16)
         square += dot(ye[e], near_y[e])
+    arrival(s0_in, 2, far).wait_recv()
+    far_s0 = (three - (far_square + s0_in[far].astype(F32)) * far_live).astype(BF16)
+    theirs = near_part[far] + dot(far_s0, toward[far])
+    near_y[far] = (0.5 * theirs * near_live[far]).astype(BF16)
+    square += dot(ye[far], near_y[far])
     last_s = (three - square * own_live[0]).astype(BF16)
+    far_following += dot(far_s0, diag[far])
     results = [dot(last_s, y0[...])] + [dot(last_s, ye[e]) for e in range(4)]
-    for e in order:
+    for e in range(4):
         arrival(y0_in, 3, e).wait_recv()
-        side = y0_ye[e] + dot(ye[e], y0_in[e])
+        theirs = y0_in[e]
+        if e == far:
+            theirs = (0.5 * (far_following + theirs.astype(F32)) * far_live).astype(BF16)
+        side = y0_ye[e] + dot(ye[e], theirs)
         side = (-side * own_live[e + 1]).astype(BF16)
         results[0] += dot(side, near_y[e])
-        results[e + 1] += dot(side, y0_in[e])
+        results[e + 1] += dot(side, theirs)
 
     stores = []
     place_id = lax.broadcasted_iota(jnp.int32, (slots, 1), 0)
@@ -232,10 +315,13 @@
             pltpu.VMEM((4,) + square, BF16),
             pltpu.VMEM(square, BF16),
             pltpu.VMEM((4,) + square, BF16),
+            pltpu.VMEM(square, BF16),
+            pltpu.VMEM(square, BF16),
             pltpu.VMEM(xvals.shape, F32),
             pltpu.SemaphoreType.DMA((7,)),
             pltpu.SemaphoreType.DMA((4, 4)),
             pltpu.SemaphoreType.DMA((4, 4)),
+            pltpu.SemaphoreType.REGULAR((4,)),
         ],
         compiler_params=pltpu.CompilerParams(
             collective_id=0, has_side_effects=True, vmem_limit_bytes=60 * 1024 * 1024

time: 38.3 us -> 36.5 us (0.953)
  the two profiles are of different devices: /device:TPU:64 before, /device:TPU:2 now
where the time goes in v2:
time: 36.5 us; the launch traced here: 36.3 us
  Pallas kernels  34.6 us (95%)
  local copies, waits for them, and re-layouts  1.72 us (5%)
    pallas_call x1, Pallas kernels, per_device(): pl.pallas_call(functools.partial(kernel, row_count, col_count, block, slo...  34.6 us
    unnamed x1, local copies, waits for them, and re-layouts  1.72 us

profile of v2, /device:TPU:2, one launch (start us, length us, event | category | flops | bytes accessed | tf_op | source)
XLA Modules:
  0.0 36.3 jit_solution(5644297932895273358)
XLA Ops:
  0.0 34.6 %sign_steps.1 = f32[2,64,640]{2,1,0:T(8,128)} custom-call(bf16[2,64,640]{2,1,0:T(8,128)(2,1)} %x_hbm.1, s32[10,2048]{1,0:T(8,128)} %bitcast.2, s32[16,128]{1,0:T(8,128)} %bitcast.3), custom_call_target="tpu_custom_call" | custom-call | flops 250000000 | bytes 600000 | tf_op jit(solution)/shard_map/sign_steps/pallas_call | solution.py:302
  34.6 1.7 %copy.5 = f32[2,64,640]{2,1,0:T(8,128)} copy(f32[2,64,640]{2,1,0:T(8,128)} %sign_steps.1) | data formatting | bytes 655360

commit v3 on v2

--- a/solution.py
+++ b/solution.py
@@ -33,20 +33,6 @@
     back = (1, 0, 2, 3)
     near, far = (0, 1, 2), 3
 
-    def rank(row, col):
-        z = lax.rem(lax.div(col, 2), 4) * 4 + lax.div(row, 4)
-        usual = (z * 64 + lax.div(col, 8)) * 8 + lax.rem(row, 4) * 2 + lax.rem(col, 2)
-        return jnp.where(row + col == 0, 12 * 512 - 1, usual)
-
-    mine = rank(r, c)
-    later = [rank(*place) > mine for place in places]
-    barrier = pltpu.get_barrier_semaphore()
-    for e in range(4):
-
-        @pl.when(later[e])
-        def _(e=e):
-            pl.semaphore_signal(barrier, inc=1, device_id=places[e], device_id_type=MESH)
-
     width = 2 * col_count
     loads = []
     for at, grid_row in enumerate((r, up, down)):
@@ -56,22 +42,22 @@
         )
     loads.append(pltpu.make_async_copy(counts_hbm, cnts, local_sem.at[3]))
     loads.append(pltpu.make_async_copy(x_hbm, xs, local_sem.at[4]))
-    for load in loads:
+    for load in loads[::-1]:
         load.start()
 
-    earlier = sum(1 - late.astype(jnp.int32) for late in later)
-
-    @pl.when(earlier > 0)
-    def _():
-        pl.semaphore_wait(barrier, earlier)
-
+    def rank(row, col):
+        z = lax.rem(lax.div(col, 2), 4) * 4 + lax.div(row, 4)
+        usual = (z * 64 + lax.div(col, 8)) * 8 + lax.rem(row, 4) * 2 + lax.rem(col, 2)
+        return jnp.where(row + col == 0, 12 * 512 - 1, usual)
+
+    mine = rank(r, c)
+    later = [rank(*place) > mine for place in places]
+    barrier = pltpu.get_barrier_semaphore()
     for e in range(4):
 
-        @pl.when(jnp.logical_not(later[e]))
+        @pl.when(later[e])
         def _(e=e):
-            pl.semaphore_signal(
-                hello.at[back[e]], inc=1, device_id=places[e], device_id_type=MESH
-            )
+            pl.semaphore_signal(barrier, inc=1, device_id=places[e], device_id_type=MESH)
 
     lane = lax.broadcasted_iota(jnp.int32, (1, pair), 1)
     second = (lane >= block).astype(jnp.int32)
@@ -91,6 +77,20 @@
         load.wait()
     own = [stored_row(0, r, c, which) for which in range(2)]
     masks = [[(own[i] == wide[g]) for g in range(5)] for i in range(2)]
+
+    earlier = sum(1 - late.astype(jnp.int32) for late in later)
+
+    @pl.when(earlier > 0)
+    def _():
+        pl.semaphore_wait(barrier, earlier)
+
+    for e in range(4):
+
+        @pl.when(jnp.logical_not(later[e]))
+        def _(e=e):
+            pl.semaphore_signal(
+                hello.at[back[e]], inc=1, device_id=places[e], device_id_type=MESH
+            )
 
     def live(parts):
         return jnp.concatenate(
@@ -156,12 +156,18 @@
 
     for e in near:
 
+        @pl.when(jnp.logical_not(later[e]))
+        def _(e=e):
+            for copy in first[e]:
+                copy.start()
+
+    for e in near[::-1]:
+
         @pl.when(later[e])
         def _(e=e):
             pl.semaphore_wait(hello.at[e], 1)
-
-        for copy in first[e]:
-            copy.start()
+            for copy in first[e]:
+                copy.start()
 
     own_live = [live([masks[i][g] for i in range(2)]) for g in range(5)]
     near_live = []

time: 36.5 us -> 35.2 us (0.964)
  the two profiles are of different devices: /device:TPU:2 before, /device:TPU:56 now
where the time goes in v3:
time: 35.2 us; the launch traced here: 35 us
  Pallas kernels  33.3 us (95%)
  local copies, waits for them, and re-layouts  1.72 us (5%)
    pallas_call x1, Pallas kernels, per_device(): pl.pallas_call(functools.partial(kernel, row_count, col_count, block, slo...  33.3 us
    unnamed x1, local copies, waits for them, and re-layouts  1.72 us

profile of v3, /device:TPU:56, one launch (start us, length us, event | category | flops | bytes accessed | tf_op | source)
XLA Modules:
  0.0 35.0 jit_solution(5453018513178000402)
XLA Ops:
  0.0 33.3 %sign_steps.1 = f32[2,64,640]{2,1,0:T(8,128)} custom-call(bf16[2,64,640]{2,1,0:T(8,128)(2,1)} %x_hbm.1, s32[10,2048]{1,0:T(8,128)} %bitcast.2, s32[16,128]{1,0:T(8,128)} %bitcast.3), custom_call_target="tpu_custom_call" | custom-call | flops 250000000 | bytes 600000 | tf_op jit(solution)/shard_map/sign_steps/pallas_call | solution.py:308
  33.3 1.7 %copy.5 = f32[2,64,640]{2,1,0:T(8,128)} copy(f32[2,64,640]{2,1,0:T(8,128)} %sign_steps.1) | data formatting | bytes 655360

commit v4 on v3

--- a/solution.py
+++ b/solution.py
@@ -18,9 +18,9 @@
 
 def kernel(
     row_count, col_count, block, slots,
-    x_hbm, cols_hbm, counts_hbm, out_hbm,
-    xs, tiles, cnts, can, toward, diag, s0, s0_in, y0, y0_in, part_a, part_b, outv,
-    local_sem, send_sem, recv_sem, hello,
+    xs, all_cols, cnts, _, out,
+    can, toward, diag, s0, s0_in, y0, y0_in, part_a, part_b,
+    send_sem, recv_sem, hello,
 ):
     pair = 2 * block
     r = lax.axis_index("row")
@@ -34,16 +34,10 @@
     near, far = (0, 1, 2), 3
 
     width = 2 * col_count
-    loads = []
-    for at, grid_row in enumerate((r, up, down)):
-        lanes = pl.ds(pl.multiple_of(grid_row * width, width), width)
-        loads.append(
-            pltpu.make_async_copy(cols_hbm.at[:, lanes], tiles.at[at], local_sem.at[at])
-        )
-    loads.append(pltpu.make_async_copy(counts_hbm, cnts, local_sem.at[3]))
-    loads.append(pltpu.make_async_copy(x_hbm, xs, local_sem.at[4]))
-    for load in loads[::-1]:
-        load.start()
+    tiles = [
+        all_cols[:, pl.ds(pl.multiple_of(grid_row * width, width), width)]
+        for grid_row in (r, up, down)
+    ]
 
     def rank(row, col):
         z = lax.rem(lax.div(col, 2), 4) * 4 + lax.div(row, 4)
@@ -73,8 +67,6 @@
         count = jnp.sum(jnp.where(here, count_row, 0.0), axis=1, keepdims=True)
         return jnp.where(slot_id < count, ids, -1.0)
 
-    for load in loads[:4]:
-        load.wait()
     own = [stored_row(0, r, c, which) for which in range(2)]
     masks = [[(own[i] == wide[g]) for g in range(5)] for i in range(2)]
 
@@ -104,7 +96,6 @@
         )
 
     first_half = lane < block
-    loads[4].wait()
     for i in range(2):
         sums = [jnp.zeros((block, pair), F32) for _ in range(5)]
         for j in range(slots // 2):
@@ -264,7 +255,6 @@
         results[0] += dot(side, near_y[e])
         results[e + 1] += dot(side, theirs)
 
-    stores = []
     place_id = lax.broadcasted_iota(jnp.int32, (slots, 1), 0)
     holder = jnp.zeros((slots, 1), jnp.int32)
     for g in range(5):
@@ -286,14 +276,13 @@
                 for j in range(slots // 2):
                     sums[j] = jnp.where(chosen[j][spot : spot + 1], doubled, sums[j])
         for j in range(slots // 2):
-            outv[i, :, j * pair : (j + 1) * pair] = sums[j]
-        store = pltpu.make_async_copy(outv.at[i], out_hbm.at[i], local_sem.at[5 + i])
-        store.start()
-        stores.append(store)
+            out[i, :, j * pair : (j + 1) * pair] = sums[j]
     for copy in sent:
         copy.wait_send()
-    for store in stores:
-        store.wait()
+
+
+def opening(out):
+    out[...] = jnp.zeros_like(out)
 
 
 def per_device(xvals, cols, counts):
@@ -304,16 +293,20 @@
     width = rows_here * col_count
     pair = 2 * block
     square = (pair, pair)
-    any_space = pl.BlockSpec(memory_space=pl.ANY)
+    inside = pl.BlockSpec(memory_space=pltpu.VMEM)
+    opened = pl.pallas_call(
+        opening,
+        out_shape=jax.ShapeDtypeStruct((8, 128), F32),
+        compiler_params=pltpu.CompilerParams(vmem_limit_bytes=1024 * 1024),
+        cost_estimate=pl.CostEstimate(flops=20000000000, bytes_accessed=20_000_000, transcendentals=0),
+        name="opening",
+    )()
     return pl.pallas_call(
         functools.partial(kernel, row_count, col_count, block, slots),
         out_shape=jax.ShapeDtypeStruct(xvals.shape, F32),
-        in_specs=[any_space] * 3,
-        out_specs=any_space,
+        in_specs=[inside] * 3 + [pl.BlockSpec(memory_space=pl.ANY)],
+        out_specs=inside,
         scratch_shapes=[
-            pltpu.VMEM(xvals.shape, BF16),
-            pltpu.VMEM((3, slots, width), jnp.int32),
-            pltpu.VMEM((row_count, width), jnp.int32),
             pltpu.VMEM((5,) + square, BF16),
             pltpu.VMEM((4,) + square, BF16),
             pltpu.VMEM((4,) + square, BF16),
@@ -323,20 +316,18 @@
             pltpu.VMEM((4,) + square, BF16),
             pltpu.VMEM(square, BF16),
             pltpu.VMEM(square, BF16),
-            pltpu.VMEM(xvals.shape, F32),
-            pltpu.SemaphoreType.DMA((7,)),
             pltpu.SemaphoreType.DMA((4, 4)),
             pltpu.SemaphoreType.DMA((4, 4)),
             pltpu.SemaphoreType.REGULAR((4,)),
         ],
         compiler_params=pltpu.CompilerParams(
-            collective_id=0, has_side_effects=True, vmem_limit_bytes=60 * 1024 * 1024
+            collective_id=0, has_side_effects=True, vmem_limit_bytes=16 * 1024 * 1024
         ),
         cost_estimate=pl.CostEstimate(
             flops=250_000_000, bytes_accessed=600_000, transcendentals=0
         ),
         name="sign_steps",
-    )(xvals, cols.T, counts.reshape(row_count, width))
+    )(xvals, cols.T, counts.reshape(row_count, width), opened)
 
 
 def solution(mesh):

time: 35.2 us -> 34.2 us (0.972)
  Pallas kernels: 33.3 us -> 32.4 us
    pallas_call x1, Pallas kernels: 33.3 us -> 32.4 us  [per_device(): pl.pallas_call(functools.partial(kernel, row_count, col_count, block, slo...]
    unnamed x1 -> x7, local copies, waits for them, and re-layouts: 1.72 us -> 1.7 us
where the time goes in v4:
time: 34.2 us; the launch traced here: 34.1 us
  Pallas kernels  32.4 us (95%)
  local copies, waits for them, and re-layouts  1.7 us (5%)
    pallas_call x1, Pallas kernels, per_device(): pl.pallas_call(functools.partial(kernel, row_count, col_count, block, slo...  32.4 us
    unnamed x7, local copies, waits for them, and re-layouts  1.7 us

profile of v4, /device:TPU:56, one launch (start us, length us, event | category | flops | bytes accessed | tf_op | source)
XLA Modules:
  0.0 34.1 jit_solution(2781540510667887950)
XLA Ops:
  0.0 0.0 copy-start
  0.0 0.0 copy-start.1
  0.0 0.0 copy-start.2
  0.0 0.9 %copy-done = bf16[2,64,640]{2,1,0:T(8,128)(2,1)S(1)} copy-done((bf16[2,64,640]{2,1,0:T(8,128)(2,1)S(1)}, bf16[2,64,640]{2,1,0:T(8,128)(2,1)}, u32[]{:S(2)}) %copy-start) | copy-done | bytes 163864
  0.9 0.1 copy-done.1
  1.0 0.0 copy-done.2
  1.0 32.4 %sign_steps.1 = f32[2,64,640]{2,1,0:T(8,128)S(1)} custom-call(bf16[2,64,640]{2,1,0:T(8,128)(2,1)S(1)} %copy-done, s32[10,2048]{1,0:T(8,128)S(1)} %bitcast.2, s32[16,128]{1,0:T(8,128)S(1)} %bitcast.3, f32[8,128]{1,0:T(8,128)S(1)} %opening.1._), custom_call_target="tpu_custom_call" | custom-call | flops 250000000 | bytes 600000 | tf_op jit(solution)/shard_map/sign_steps/pallas_call | solution.py:304
  33.3 0.7 %copy.5 = f32[2,64,640]{2,1,0:T(8,128)} copy(f32[2,64,640]{2,1,0:T(8,128)S(1)} %sign_steps.1) | data formatting | bytes 655360
  (1 shorter events, 0.0 us)
Async XLA Ops:
  0.0 0.9 %copy-start = (bf16[2,64,640]{2,1,0:T(8,128)(2,1)S(1)}, bf16[2,64,640]{2,1,0:T(8,128)(2,1)}, u32[]{:S(2)}) copy-start(bf16[2,64,640]{2,1,0:T(8,128)(2,1)} %xs.1) | copy-start | bytes 491524
  0.0 1.0 %copy-start.1 = (s32[2048,10]{0,1:T(8,128)S(1)}, s32[2048,10]{0,1:T(8,128)}, u32[]{:S(2)}) copy-start(s32[2048,10]{0,1:T(8,128)} %param.4) | copy-start | bytes 245764
  0.0 1.0 %copy-start.2 = (s32[2048]{0:T(1024)S(1)}, s32[2048]{0:T(1024)}, u32[]{:S(2)}) copy-start(s32[2048]{0:T(1024)} %param.5) | copy-start | bytes 24580

commit v5 on v4

--- a/solution.py
+++ b/solution.py
@@ -96,20 +96,6 @@
         )
 
     first_half = lane < block
-    for i in range(2):
-        sums = [jnp.zeros((block, pair), F32) for _ in range(5)]
-        for j in range(slots // 2):
-            both = xs[i, :, j * pair : (j + 1) * pair].astype(F32)
-            turned = pltpu.roll(both, block, 1)
-            for slot, doubled in (
-                (2 * j, jnp.where(first_half, both, turned)),
-                (2 * j + 1, jnp.where(first_half, turned, both)),
-            ):
-                for g in range(5):
-                    sums[g] = jnp.where(masks[i][g][slot : slot + 1], doubled, sums[g])
-        for g in range(5):
-            can[g, i * block : (i + 1) * block, :] = sums[g].astype(BF16)
-
     sent = []
 
     def post(src, dst, kind, e):
@@ -140,11 +126,30 @@
     sums_a = post(part_a, s0_in, 2, far)
     sums_b = post(part_b, y0_in, 3, far)
 
+    def arrange(groups):
+        for i in range(2):
+            sums = [jnp.zeros((block, pair), F32) for _ in groups]
+            for j in range(slots // 2):
+                both = xs[i, :, j * pair : (j + 1) * pair].astype(F32)
+                turned = pltpu.roll(both, block, 1)
+                for slot, doubled in (
+                    (2 * j, jnp.where(first_half, both, turned)),
+                    (2 * j + 1, jnp.where(first_half, turned, both)),
+                ):
+                    for k, g in enumerate(groups):
+                        chosen = masks[i][g][slot : slot + 1]
+                        sums[k] = jnp.where(chosen, doubled, sums[k])
+            for k, g in enumerate(groups):
+                can[g, i * block : (i + 1) * block, :] = sums[k].astype(BF16)
+
+    arrange((far + 1, 0))
+
     @pl.when(jnp.logical_not(later[far]))
     def _():
         for copy in first[far]:
             copy.start()
 
+    arrange((1, 2, 3))
     for e in near:
 
         @pl.when(jnp.logical_not(later[e]))
@@ -198,17 +203,10 @@
     def _():
         sums_b.start()
 
-    @pl.when(later[far])
-    def _():
-        pl.semaphore_wait(hello.at[far], 1)
-        for copy in first[far] + [sums_a, sums_b]:
-            copy.start()
-
-
     arrival(toward, 0, far).wait_recv()
     square += dot(xe[far], toward[far])
     s0[...] = (three - square * own_live[0]).astype(BF16)
-    for e in near:
+    for e in (1, 0, 2):
         post(s0, s0_in, 2, e).start()
     added = dot(s0[...], x0)
     arrival(diag, 1, far).wait_recv()
@@ -216,8 +214,15 @@
     side_s[far] = (-side * own_live[far + 1]).astype(BF16)
     added += dot(side_s[far], toward[far])
     y0[...] = (0.5 * (following + added) * own_live[0]).astype(BF16)
-    for e in near:
+    for e in (1, 0, 2):
         post(y0, y0_in, 3, e).start()
+
+    @pl.when(later[far])
+    def _():
+        pl.semaphore_wait(hello.at[far], 1)
+        for copy in first[far] + [sums_a, sums_b]:
+            copy.start()
+
 
     ye = []
     near_part = []
@@ -232,7 +237,7 @@
     square = dot(y0[...], y0[...])
     y0_ye = [dot(y0[...], ye[e]) for e in range(4)]
     near_y = [None] * 4
-    for e in near:
+    for e in (1, 2):
         arrival(s0_in, 2, e).wait_recv()
         theirs = near_part[e] + dot(s0_in[e], toward[e])
         near_y[e] = (0.5 * theirs * near_live[e]).astype(BF16)
@@ -242,10 +247,15 @@
     theirs = near_part[far] + dot(far_s0, toward[far])
     near_y[far] = (0.5 * theirs * near_live[far]).astype(BF16)
     square += dot(ye[far], near_y[far])
+    far_following += dot(far_s0, diag[far])
+    for e in (0,):
+        arrival(s0_in, 2, e).wait_recv()
+        theirs = near_part[e] + dot(s0_in[e], toward[e])
+        near_y[e] = (0.5 * theirs * near_live[e]).astype(BF16)
+        square += dot(ye[e], near_y[e])
     last_s = (three - square * own_live[0]).astype(BF16)
-    far_following += dot(far_s0, diag[far])
     results = [dot(last_s, y0[...])] + [dot(last_s, ye[e]) for e in range(4)]
-    for e in range(4):
+    for e in (1, 2, 3, 0):
         arrival(y0_in, 3, e).wait_recv()
         theirs = y0_in[e]
         if e == far:

time: 34.2 us -> 33.7 us (0.985)
  Pallas kernels: 32.4 us -> 31.6 us
    pallas_call x1, Pallas kernels: 32.4 us -> 31.6 us  [per_device(): pl.pallas_call(functools.partial(kernel, row_count, col_count, block, slo...]
where the time goes in v5:
time: 33.7 us; the launch traced here: 33.4 us
  Pallas kernels  31.6 us (94%)
  local copies, waits for them, and re-layouts  1.7 us (5%)
    pallas_call x1, Pallas kernels, per_device(): pl.pallas_call(functools.partial(kernel, row_count, col_count, block, slo...  31.6 us
    unnamed x7, local copies, waits for them, and re-layouts  1.7 us

profile of v5, /device:TPU:56, one launch (start us, length us, event | category | flops | bytes accessed | tf_op | source)
XLA Modules:
  0.0 33.4 jit_solution(10559104277775377858)
XLA Ops:
  0.0 0.0 copy-start
  0.0 0.0 copy-start.1
  0.0 0.0 copy-start.2
  0.0 0.9 %copy-done = bf16[2,64,640]{2,1,0:T(8,128)(2,1)S(1)} copy-done((bf16[2,64,640]{2,1,0:T(8,128)(2,1)S(1)}, bf16[2,64,640]{2,1,0:T(8,128)(2,1)}, u32[]{:S(2)}) %copy-start) | copy-done | bytes 163864
  0.9 0.1 copy-done.1
  1.0 0.0 copy-done.2
  1.0 31.6 %sign_steps.1 = f32[2,64,640]{2,1,0:T(8,128)S(1)} custom-call(bf16[2,64,640]{2,1,0:T(8,128)(2,1)S(1)} %copy-done, s32[10,2048]{1,0:T(8,128)S(1)} %bitcast.2, s32[16,128]{1,0:T(8,128)S(1)} %bitcast.3, f32[8,128]{1,0:T(8,128)S(1)} %opening.1._), custom_call_target="tpu_custom_call" | custom-call | flops 250000000 | bytes 600000 | tf_op jit(solution)/shard_map/sign_steps/pallas_call | solution.py:314
  32.6 0.7 %copy.5 = f32[2,64,640]{2,1,0:T(8,128)} copy(f32[2,64,640]{2,1,0:T(8,128)S(1)} %sign_steps.1) | data formatting | bytes 655360
  (1 shorter events, 0.0 us)
Async XLA Ops:
  0.0 0.9 %copy-start = (bf16[2,64,640]{2,1,0:T(8,128)(2,1)S(1)}, bf16[2,64,640]{2,1,0:T(8,128)(2,1)}, u32[]{:S(2)}) copy-start(bf16[2,64,640]{2,1,0:T(8,128)(2,1)} %xs.1) | copy-start | bytes 491524
  0.0 1.0 %copy-start.1 = (s32[2048,10]{0,1:T(8,128)S(1)}, s32[2048,10]{0,1:T(8,128)}, u32[]{:S(2)}) copy-start(s32[2048,10]{0,1:T(8,128)} %param.4) | copy-start | bytes 245764
  0.0 1.0 %copy-start.2 = (s32[2048]{0:T(1024)S(1)}, s32[2048]{0:T(1024)}, u32[]{:S(2)}) copy-start(s32[2048]{0:T(1024)} %param.5) | copy-start | bytes 24580
